TPU v7x, 32 devices: a whole 2x2x4 slice. The times are simulated.
32 devices in a mesh: grp: 2 (over x), gx: 16 (over z, y, core).
Axes of the slice: x: 2, y: 2, z: 4, core: 2. Of those that a mesh axis runs over, the one named last changes fastest.
Arguments:
- field: float32 [32, 1024, 1024], P('grp', 'gx'), parts along dimension 0, may hold values from -150 to 150
- basis_one: float32 [2048, 256], P('grp'), parts along dimension 0, may hold values from -0.1875 to 0.1875
- start: float32 [1024, 256], replicated, may hold values from -6 to 6
Outputs:
- basis_two: float32 [2048, 256], P('grp'), parts along dimension 0
- core: float32 [32, 256, 256], P(('grp', 'gx')), parts along dimension 0
There are 2 independent parts, one for each index of `grp`. A program takes and returns all parts, laid end to end along the dimension named above; an argument that names none is the same for every part. Nothing has to cross between parts.
All inputs are finite; a program needn't handle non-finite values.
Results may differ from a plain program's by a relative error of at most 0.0003.
Values sent between devices are 32-bit elements; how exact they have to be, the bound alone decides.
A program may use at most 128 MiB of HBM per device.

v0:
```python
import jax
import jax.numpy as jnp
from jax import lax
from jax.sharding import PartitionSpec as P

ITERS = 4


def body(field, basis_one, start):
    highest = lax.Precision.HIGHEST
    fibred = lax.all_to_all(field, "gx", split_axis=2, concat_axis=1, tiled=True)
    fibred = jnp.swapaxes(fibred, 1, 2)
    partial_comp = jnp.einsum("ir,kji->kjr", basis_one, fibred, precision=highest)
    compressed = lax.all_to_all(partial_comp, "gx", split_axis=0, concat_axis=1, tiled=True)
    partial_gram = jnp.einsum("kir,kjr->ij", compressed, compressed, precision=highest)
    gram = lax.psum(partial_gram, "gx")
    iterate = start
    for step in range(ITERS):
        product = jnp.dot(gram, iterate, precision=highest)
        cross = jnp.dot(product.T, product, precision=highest)
        factor = jnp.linalg.cholesky(cross)
        iterate = jax.scipy.linalg.solve_triangular(factor, product.T, lower=True).T
    core = jnp.einsum("kjr,js->krs", compressed, iterate, precision=highest)
    return (iterate, core)


def solution(mesh):
    in_specs = (P("grp", "gx", None), P("grp", None), P())
    out_specs = (P("grp", None), P(("grp", "gx"), None, None))
    return jax.shard_map(body, mesh=mesh, in_specs=in_specs, out_specs=out_specs, check_vma=False)
```

profile of v0, /device:TPU:0, one launch (start us, length us, event | category | flops | bytes accessed | tf_op | source)
XLA Modules:
  0.0 612.4 jit_solution(4899606233928193867)
XLA Ops:
  7.2 8.2 %copy.11 = f32[16,64,1024]{1,0,2:T(8,128)} copy(f32[16,64,1024]{2,1,0:T(8,128)} %param.6) | data formatting | bytes 8388608 | tf_op args[0]
  15.4 13.3 %reshape.61 = f32[16,1,65536]{2,1,0:T(1,128)} reshape(f32[1024,16,64]{2,1,0:T(8,128)} %bitcast.165) | data formatting | bytes 8388608
  28.7 99.7 %all_to_all.27 = f32[16,1,65536]{2,1,0:T(1,128)} all-to-all(f32[16,1,65536]{2,1,0:T(1,128)} %reshape.61), channel_id=1, replica_groups=mesh['grp'=2,'gx'=16] {'gx'}, dimensions={0} | all-to-all | bytes 8388608 | tf_op jit(solution)/shard_map/all_to_all | solution.py:11
  128.9 13.7 %reduce.8 = f32[16,65536]{1,0:T(8,128)} reduce(f32[16,1,65536]{2,1,0:T(1,128)} %all_to_all.27, f32[]{:T(128)} %broadcast.91), dimensions={1}, to_apply=%all_to_all.20.reduce_sub_computation | reduce | bytes 8388612 | tf_op jit(solution)/shard_map/all_to_all | solution.py:11
  142.7 6.9 %reshape.62 = f32[1024,16,64]{2,1,0:T(8,128)} reshape(f32[16,65536]{1,0:T(8,128)} %reduce.8) | data formatting | bytes 8388608
  149.6 11.4 %copy.19 = f32[16,64,16,64]{1,2,3,0:T(8,128)} copy(f32[16,64,16,64]{1,0,3,2:T(8,128)} %bitcast.166) | data formatting | bytes 8388608 | tf_op jit(solution)/shard_map/all_to_all | solution.py:11
  161.0 7.6 %all_to_all.23 = f32[16,1024,64]{1,2,0:T(8,128)} reshape(f32[16,16,64,64]{2,1,3,0:T(8,128)} %bitcast.167) | data formatting | bytes 8388608 | tf_op jit(solution)/shard_map/all_to_all | solution.py:11
  168.6 5.5 fusion
  174.1 30.4 %all_to_all.28 = f32[16,64,256]{2,1,0:T(8,128)S(1)} all-to-all(f32[16,64,256]{2,1,0:T(8,128)S(1)} %fusion), channel_id=1, replica_groups=mesh['grp'=2,'gx'=16] {'gx'}, dimensions={0} | all-to-all | bytes 2097152 | tf_op jit(solution)/shard_map/all_to_all | solution.py:14
  204.5 5.1 fusion.68
  209.6 111.9 %all-reduce.3.cloned.1.call-done = f32[1024,1024]{1,0:T(8,128)} async-done(((f32[1024,1024]{1,0:T(8,128)}), f32[1024,1024]{1,0:T(8,128)}) %all-reduce.3.cloned.1.call-update) | async-done | bytes 4194320 | tf_op jit(solution)/shard_map/psum | solution.py:16
  321.6 5.2 fusion.69
  326.8 1.8 fusion.70
  328.8 11.7 %cholesky.214 = f32[128,128]{1,0:T(8,128)S(1)} custom-call(f32[128,128]{1,0:T(8,128)S(1)} %cholesky.346), custom_call_target="Cholesky" | custom-call | tf_op jit(solution)/shard_map/jit(cholesky)/cholesky | solution.py:21
  340.6 9.8 %custom-call.17 = f32[1,128,128]{1,2,0:T(8,128)S(1)} custom-call(f32[1,128,128]{2,1,0:T(8,128)S(1)} %get-tuple-element.93), custom_call_target="InvertDiagBlocksLowerTriangular" | custom-call | tf_op jit(solution)/shard_map/jit(cholesky)/cholesky | solution.py:21
  350.9 11.7 %cholesky.231 = f32[128,128]{1,0:T(8,128)S(1)} custom-call(f32[128,128]{1,0:T(8,128)S(1)} %convolution_subtract_fusion.7), custom_call_target="Cholesky" | custom-call | tf_op jit(solution)/shard_map/jit(cholesky)/cholesky | solution.py:21
  362.7 0.7 compare_reduce_fusion.6
  364.9 3.9 while.8
  365.5 1.3 bitcast_dynamic-update-slice_fusion.8
  367.4 1.3 bitcast_dynamic-update-slice_fusion.8
  368.7 19.7 %custom-call.18 = f32[2,128,128]{1,2,0:T(8,128)S(1)} custom-call(f32[2,128,128]{2,1,0:T(8,128)S(1)} %get-tuple-element.30), custom_call_target="InvertDiagBlocksLowerTriangular" | custom-call | tf_op jit(solution)/shard_map/jit(_solve_triangular)/triangular_solve | solution.py:22
  388.4 0.6 fusion.22
  389.1 1.0 convolution_subtract_fusion.3
  390.1 0.6 fusion.41
  390.7 5.3 fusion.2
  396.1 1.8 fusion.71
  398.1 11.7 %cholesky.248 = f32[128,128]{1,0:T(8,128)S(1)} custom-call(f32[128,128]{1,0:T(8,128)S(1)} %cholesky.349), custom_call_target="Cholesky" | custom-call | tf_op jit(solution)/shard_map/jit(cholesky)/cholesky | solution.py:21
  409.9 9.8 %custom-call.19 = f32[1,128,128]{1,2,0:T(8,128)S(1)} custom-call(f32[1,128,128]{2,1,0:T(8,128)S(1)} %get-tuple-element.89), custom_call_target="InvertDiagBlocksLowerTriangular" | custom-call | tf_op jit(solution)/shard_map/jit(cholesky)/cholesky | solution.py:21
  420.2 11.7 %cholesky.265 = f32[128,128]{1,0:T(8,128)S(1)} custom-call(f32[128,128]{1,0:T(8,128)S(1)} %convolution_subtract_fusion.6), custom_call_target="Cholesky" | custom-call | tf_op jit(solution)/shard_map/jit(cholesky)/cholesky | solution.py:21
  431.9 0.6 compare_reduce_fusion.4
  434.9 3.9 while.9
  435.5 1.4 bitcast_dynamic-update-slice_fusion.9
  437.5 1.4 bitcast_dynamic-update-slice_fusion.9
  438.9 19.7 %custom-call.20 = f32[2,128,128]{1,2,0:T(8,128)S(1)} custom-call(f32[2,128,128]{2,1,0:T(8,128)S(1)} %get-tuple-element.31), custom_call_target="InvertDiagBlocksLowerTriangular" | custom-call | tf_op jit(solution)/shard_map/jit(_solve_triangular)/triangular_solve | solution.py:22
  458.6 0.6 fusion.20
  459.2 1.0 convolution_subtract_fusion.2
  460.2 0.6 fusion.37
  460.9 5.5 fusion.6
  466.4 1.8 fusion.72
  468.4 11.7 %cholesky.282 = f32[128,128]{1,0:T(8,128)S(1)} custom-call(f32[128,128]{1,0:T(8,128)S(1)} %cholesky.352), custom_call_target="Cholesky" | custom-call | tf_op jit(solution)/shard_map/jit(cholesky)/cholesky | solution.py:21
  480.2 9.8 %custom-call.21 = f32[1,128,128]{1,2,0:T(8,128)S(1)} custom-call(f32[1,128,128]{2,1,0:T(8,128)S(1)} %get-tuple-element.85), custom_call_target="InvertDiagBlocksLowerTriangular" | custom-call | tf_op jit(solution)/shard_map/jit(cholesky)/cholesky | solution.py:21
  490.5 11.7 %cholesky.299 = f32[128,128]{1,0:T(8,128)S(1)} custom-call(f32[128,128]{1,0:T(8,128)S(1)} %convolution_subtract_fusion.5), custom_call_target="Cholesky" | custom-call | tf_op jit(solution)/shard_map/jit(cholesky)/cholesky | solution.py:21
  502.2 0.6 compare_reduce_fusion.2
  505.2 3.9 while.10
  505.9 1.4 bitcast_dynamic-update-slice_fusion.10
  507.8 1.4 bitcast_dynamic-update-slice_fusion.10
  509.2 19.7 %custom-call.22 = f32[2,128,128]{1,2,0:T(8,128)S(1)} custom-call(f32[2,128,128]{2,1,0:T(8,128)S(1)} %get-tuple-element.32), custom_call_target="InvertDiagBlocksLowerTriangular" | custom-call | tf_op jit(solution)/shard_map/jit(_solve_triangular)/triangular_solve | solution.py:22
  528.9 0.6 fusion.18
  529.5 1.0 convolution_subtract_fusion.1
  530.5 0.6 fusion.33
  531.2 5.3 fusion.10
  536.5 1.8 fusion.73
  538.5 11.7 %cholesky.316 = f32[128,128]{1,0:T(8,128)S(1)} custom-call(f32[128,128]{1,0:T(8,128)S(1)} %cholesky.355), custom_call_target="Cholesky" | custom-call | tf_op jit(solution)/shard_map/jit(cholesky)/cholesky | solution.py:21
  550.3 9.8 %custom-call.23 = f32[1,128,128]{1,2,0:T(8,128)S(1)} custom-call(f32[1,128,128]{2,1,0:T(8,128)S(1)} %get-tuple-element.81), custom_call_target="InvertDiagBlocksLowerTriangular" | custom-call | tf_op jit(solution)/shard_map/jit(cholesky)/cholesky | solution.py:21
  560.6 11.7 %cholesky.333 = f32[128,128]{1,0:T(8,128)S(1)} custom-call(f32[128,128]{1,0:T(8,128)S(1)} %convolution_subtract_fusion.4), custom_call_target="Cholesky" | custom-call | tf_op jit(solution)/shard_map/jit(cholesky)/cholesky | solution.py:21
  572.4 0.7 compare_reduce_fusion
  575.3 4.1 while.11
  575.9 1.4 bitcast_dynamic-update-slice_fusion.11
  578.0 1.4 bitcast_dynamic-update-slice_fusion.11
  579.4 19.7 %custom-call.24 = f32[2,128,128]{1,2,0:T(8,128)S(1)} custom-call(f32[2,128,128]{2,1,0:T(8,128)S(1)} %get-tuple-element.33), custom_call_target="InvertDiagBlocksLowerTriangular" | custom-call | tf_op jit(solution)/shard_map/jit(_solve_triangular)/triangular_solve | solution.py:22
  599.7 1.0 convolution_subtract_fusion
  600.7 0.6 fusion.29
  601.4 2.5 convolution_bitcast_fusion
  604.0 1.3 copy.17
  (72 shorter events, 12.1 us)
Async XLA Ops:
  7.2 161.5 %copy-start = (f32[1024,256]{1,0:T(8,128)S(1)}, f32[1024,256]{1,0:T(8,128)}, u32[]{:S(2)}) copy-start(f32[1024,256]{1,0:T(8,128)} %param.7) | copy-start | bytes 3145732
  7.2 314.4 %all-reduce.3.cloned.1.call-start = ((), (), s32[]{:S(2)}) async-start(), calls=%async_computation.2 | async-start | bytes 8388608 | tf_op jit(solution)/shard_map/psum | solution.py:16
  204.5 117.0 %copy-start.2 = (f32[1024,256]{1,0:T(8,128)S(1)}, f32[1024,256]{1,0:T(8,128)}, u32[]{:S(2)}) copy-start(f32[1024,256]{1,0:T(8,128)} %param.8) | copy-start | bytes 3145732
  599.7 5.6 copy-start.1
Sparse Core Ops, SparseCore 0:
  209.7 111.7 all-reduce.2
where the time goes:
time: 622 us; the launch traced here: 612 us
  other arithmetic  232 us (37%)
  blocking collectives  130 us (21%)
  waiting for transfers between devices  112 us (18%)
  local copies, waits for them, and re-layouts  65.6 us (11%)
  matrix products  52.8 us (8%)
  between operations  20 us (3%)
    another operation x27, other arithmetic, body(): factor = jnp.linalg.cholesky(cross)  138 us
    psum x1, waiting for transfers between devices, body(): gram = lax.psum(partial_gram, 'gx')  112 us
    all_to_all x1, blocking collectives, body(): lax.all_to_all(field, 'gx', split_axis=2, concat_axis=1, tiled=True)  99.7 us
    another operation x9, other arithmetic, body(): iterate = jax.scipy.linalg.solve_triangular(factor, product.T, lower=True).T  79.8 us
    all_to_all x1, blocking collectives, body(): lax.all_to_all(partial_comp, 'gx', split_axis=0, concat_axis=1, tiled=True)  30.4 us
    unnamed x10, local copies, waits for them, and re-layouts  29.7 us
    dot_general x4, matrix products, body(): product = jnp.dot(gram, iterate, precision=highest)  21.4 us
    all_to_all x3, local copies, waits for them, and re-layouts, body(): lax.all_to_all(field, 'gx', split_axis=2, concat_axis=1, tiled=True)  19.6 us
  transfers between devices with their start and end apart: 1, of which 1 were waited for; matrix products, arithmetic and copies ran while one was open for 0% of the time, Pallas kernels for 0%

commit v1 on v0

v1 whole, which is shorter than its diff:
```python
import jax
import jax.numpy as jnp
from jax import lax
from jax.sharding import PartitionSpec as P

ITERS = 4
BLOCK = 128
HIGHEST = lax.Precision.HIGHEST


def packed_gram(compressed):
    width = compressed.shape[2]
    rows = [
        jnp.einsum("kri,krj->ij", compressed[:, :, at:at + BLOCK], compressed[:, :, at:], precision=HIGHEST)
        for at in range(0, width, BLOCK)
    ]
    return jnp.concatenate(rows, axis=1)


def unpacked_gram(packed, width):
    rows, offset = [], 0
    for at in range(0, width, BLOCK):
        rows.append(packed[:, offset:offset + width - at])
        offset += width - at
    whole = []
    for a in range(len(rows)):
        below = [rows[b][:, (a - b) * BLOCK:(a - b + 1) * BLOCK].T for b in range(a)]
        whole.append(jnp.concatenate(below + [rows[a]], axis=1))
    return jnp.concatenate(whole, axis=0)


def body(field, basis_one, start):
    planes = lax.all_to_all(field, "gx", split_axis=0, concat_axis=1, tiled=True)
    compressed = jnp.einsum("ir,kij->krj", basis_one, planes, precision=HIGHEST)
    gram = unpacked_gram(lax.psum(packed_gram(compressed), "gx"), compressed.shape[2])
    iterate = start
    for step in range(ITERS):
        product = jnp.dot(gram, iterate, precision=HIGHEST)
        cross = jnp.dot(product.T, product, precision=HIGHEST)
        factor = jnp.linalg.cholesky(cross)
        iterate = jax.scipy.linalg.solve_triangular(factor, product.T, lower=True).T
    core = jnp.einsum("krj,js->krs", compressed, iterate, precision=HIGHEST)
    return (iterate, core)


def solution(mesh):
    in_specs = (P("grp", "gx", None), P("grp", None), P())
    out_specs = (P("grp", None), P(("grp", "gx"), None, None))
    return jax.shard_map(body, mesh=mesh, in_specs=in_specs, out_specs=out_specs, check_vma=False)
```

time: 622 us -> 595 us (0.957)
  blocking collectives: 130 us -> 99.8 us
  matrix products: 52.8 us -> 65.9 us
  waiting for transfers between devices: 112 us -> 99.9 us
    all_to_all x2 -> x1, blocking collectives: 130 us -> 99.8 us  [body(): lax.all_to_all(field, 'gx', split_axis=0, concat_axis=1, tiled=True)]
    all_to_all x3 -> x0, local copies, waits for them, and re-layouts: 19.6 us -> none  [body(): lax.all_to_all(field, 'gx', split_axis=2, concat_axis=1, tiled=True)]
    unnamed x10 -> x131, local copies, waits for them, and re-layouts: 29.7 us -> 44 us
    all_to_all x1 -> x0, other arithmetic: 13.7 us -> none  [body(): lax.all_to_all(field, 'gx', split_axis=2, concat_axis=1, tiled=True)]
    psum x1, waiting for transfers between devices: 112 us -> 99.9 us  [body(): lax.psum(packed_gram(compressed), 'gx')]
    another operation x8, matrix products: 1.89 us -> 8.61 us  [body(): factor = jnp.linalg.cholesky(cross)]
    dot_general x11 -> x18, matrix products: 41.8 us -> 48.2 us  [the longest x4 20 us: body(): product = jnp.dot(gram, iterate, precision=HIGHEST)]
where the time goes in v1:
time: 595 us; the launch traced here: 584 us
  other arithmetic  230 us (39%)
  waiting for transfers between devices  99.9 us (17%)
  blocking collectives  99.8 us (17%)
  local copies, waits for them, and re-layouts  66.9 us (11%)
  matrix products  65.9 us (11%)
  between operations  21.1 us (4%)
    another operation x27, other arithmetic, body(): factor = jnp.linalg.cholesky(cross)  138 us
    psum x1, waiting for transfers between devices, body(): lax.psum(packed_gram(compressed), 'gx')  99.9 us
    all_to_all x1, blocking collectives, body(): lax.all_to_all(field, 'gx', split_axis=0, concat_axis=1, tiled=True)  99.8 us
    another operation x9, other arithmetic, body(): iterate = jax.scipy.linalg.solve_triangular(factor, product.T, lower=True).T  85.9 us
    unnamed x131, local copies, waits for them, and re-layouts  44 us
    dot_general x4, matrix products, body(): product = jnp.dot(gram, iterate, precision=HIGHEST)  20 us
    another operation x29, local copies, waits for them, and re-layouts, body(): iterate = jax.scipy.linalg.solve_triangular(factor, product.T, lower=True).T  15.9 us
  transfers between devices with their start and end apart: 1, of which 1 were waited for; matrix products, arithmetic and copies ran while one was open for 0% of the time, Pallas kernels for 0%

profile of v1, /device:TPU:0, one launch (start us, length us, event | category | flops | bytes accessed | tf_op | source)
XLA Modules:
  0.0 584.0 jit_solution(16864948717030806475)
XLA Ops:
  7.2 99.8 %all_to_all.4 = f32[16,64,1024]{2,1,0:T(8,128)S(1)} all-to-all(f32[16,64,1024]{2,1,0:T(8,128)} %param.6), channel_id=1, replica_groups=mesh['grp'=2,'gx'=16] {'gx'}, dimensions={0} | all-to-all | bytes 8388608 | tf_op jit(solution)/shard_map/all_to_all | solution.py:33
  107.0 6.9 %fusion.69 = f32[1024,256]{1,0:T(8,128)S(1)} fusion(f32[1024,1024]{1,0:T(8,128)S(1)} %bitcast.257, f32[1024,256]{1,0:T(8,128)S(1)} %copy-done), kind=kOutput, calls=%fused_computation.181 | convolution fusion | flops 3221225472 | bytes 6291456 | tf_op jit(solution)/shard_map/ir,kij->krj/dot_general | solution.py:34
  113.9 2.0 convolution_dynamic-update-slice_fusion
  115.9 1.7 convolution_dynamic-update-slice_fusion.1
  117.7 1.7 convolution_dynamic-update-slice_fusion.2
  119.3 1.5 convolution_dynamic-update-slice_fusion.3
  125.4 99.9 %all-reduce.3.cloned.1.call-done = f32[128,4608]{1,0:T(8,128)} async-done(((f32[128,4608]{1,0:T(8,128)}), f32[128,4608]{1,0:T(8,128)}) %all-reduce.3.cloned.1.call-update) | async-done | bytes 2359312 | tf_op jit(solution)/shard_map/psum | solution.py:35
  230.5 2.4 fusion.67
  232.9 1.6 copy.49
  234.5 1.6 copy.50
  236.1 1.6 copy.51
  237.7 1.7 copy.52
  239.4 1.6 copy.53
  240.9 1.6 copy.54
  242.5 1.6 copy.55
  244.0 1.6 copy.56
  245.6 1.5 copy.57
  247.1 1.6 copy.58
  248.7 1.6 copy.59
  250.3 1.6 copy.60
  251.8 1.6 copy.61
  253.4 1.6 copy.62
  254.9 1.6 copy.63
  256.5 1.6 copy.64
  258.0 1.6 copy.65
  259.6 1.6 copy.66
  261.2 1.6 copy.67
  266.8 1.9 copy-done.1
  268.7 3.4 fusion.70
  272.2 1.8 fusion.71
  276.5 11.7 %cholesky.214 = f32[128,128]{1,0:T(8,128)S(1)} custom-call(f32[128,128]{1,0:T(8,128)S(1)} %cholesky.346), custom_call_target="Cholesky" | custom-call | tf_op jit(solution)/shard_map/jit(cholesky)/cholesky | solution.py:40
  288.3 10.3 %custom-call.17 = f32[1,128,128]{1,2,0:T(8,128)S(1)} custom-call(f32[1,128,128]{2,1,0:T(8,128)S(1)} %get-tuple-element.119), custom_call_target="InvertDiagBlocksLowerTriangular" | custom-call | tf_op jit(solution)/shard_map/jit(cholesky)/cholesky | solution.py:40
  300.7 11.7 %cholesky.231 = f32[128,128]{1,0:T(8,128)S(1)} custom-call(f32[128,128]{1,0:T(8,128)S(1)} %convolution_subtract_fusion.7), custom_call_target="Cholesky" | custom-call | tf_op jit(solution)/shard_map/jit(cholesky)/cholesky | solution.py:40
  315.5 4.0 while.8
  316.1 1.4 bitcast_dynamic-update-slice_fusion.30
  318.1 1.4 bitcast_dynamic-update-slice_fusion.30
  320.2 20.5 %custom-call.18 = f32[2,128,128]{1,2,0:T(8,128)S(1)} custom-call(f32[2,128,128]{2,1,0:T(8,128)} %copy-done.35), custom_call_target="InvertDiagBlocksLowerTriangular" | custom-call | tf_op jit(solution)/shard_map/jit(_solve_triangular)/triangular_solve | solution.py:41
  343.0 5.5 fusion
  348.5 1.8 fusion.72
  352.9 11.7 %cholesky.248 = f32[128,128]{1,0:T(8,128)S(1)} custom-call(f32[128,128]{1,0:T(8,128)S(1)} %cholesky.349), custom_call_target="Cholesky" | custom-call | tf_op jit(solution)/shard_map/jit(cholesky)/cholesky | solution.py:40
  364.6 9.8 %custom-call.19 = f32[1,128,128]{1,2,0:T(8,128)S(1)} custom-call(f32[1,128,128]{2,1,0:T(8,128)S(1)} %get-tuple-element.115), custom_call_target="InvertDiagBlocksLowerTriangular" | custom-call | tf_op jit(solution)/shard_map/jit(cholesky)/cholesky | solution.py:40
  376.6 11.7 %cholesky.265 = f32[128,128]{1,0:T(8,128)S(1)} custom-call(f32[128,128]{1,0:T(8,128)S(1)} %convolution_subtract_fusion.6), custom_call_target="Cholesky" | custom-call | tf_op jit(solution)/shard_map/jit(cholesky)/cholesky | solution.py:40
  392.0 4.0 while.9
  392.6 1.4 bitcast_dynamic-update-slice_fusion.31
  394.6 1.4 bitcast_dynamic-update-slice_fusion.31
  396.6 20.5 %custom-call.20 = f32[2,128,128]{1,2,0:T(8,128)S(1)} custom-call(f32[2,128,128]{2,1,0:T(8,128)} %copy-done.36), custom_call_target="InvertDiagBlocksLowerTriangular" | custom-call | tf_op jit(solution)/shard_map/jit(_solve_triangular)/triangular_solve | solution.py:41
  419.4 5.7 fusion.4
  425.2 1.8 fusion.73
  429.6 11.7 %cholesky.282 = f32[128,128]{1,0:T(8,128)S(1)} custom-call(f32[128,128]{1,0:T(8,128)S(1)} %cholesky.352), custom_call_target="Cholesky" | custom-call | tf_op jit(solution)/shard_map/jit(cholesky)/cholesky | solution.py:40
  441.3 9.8 %custom-call.21 = f32[1,128,128]{1,2,0:T(8,128)S(1)} custom-call(f32[1,128,128]{2,1,0:T(8,128)S(1)} %get-tuple-element.111), custom_call_target="InvertDiagBlocksLowerTriangular" | custom-call | tf_op jit(solution)/shard_map/jit(cholesky)/cholesky | solution.py:40
  453.3 11.7 %cholesky.299 = f32[128,128]{1,0:T(8,128)S(1)} custom-call(f32[128,128]{1,0:T(8,128)S(1)} %convolution_subtract_fusion.5), custom_call_target="Cholesky" | custom-call | tf_op jit(solution)/shard_map/jit(cholesky)/cholesky | solution.py:40
  468.8 4.0 while.10
  469.4 1.4 bitcast_dynamic-update-slice_fusion.32
  471.4 1.4 bitcast_dynamic-update-slice_fusion.32
  473.5 20.5 %custom-call.22 = f32[2,128,128]{1,2,0:T(8,128)S(1)} custom-call(f32[2,128,128]{2,1,0:T(8,128)} %copy-done.37), custom_call_target="InvertDiagBlocksLowerTriangular" | custom-call | tf_op jit(solution)/shard_map/jit(_solve_triangular)/triangular_solve | solution.py:41
  496.3 5.3 fusion.8
  501.6 1.8 fusion.74
  506.0 11.7 %cholesky.316 = f32[128,128]{1,0:T(8,128)S(1)} custom-call(f32[128,128]{1,0:T(8,128)S(1)} %cholesky.355), custom_call_target="Cholesky" | custom-call | tf_op jit(solution)/shard_map/jit(cholesky)/cholesky | solution.py:40
  517.8 9.8 %custom-call.23 = f32[1,128,128]{1,2,0:T(8,128)S(1)} custom-call(f32[1,128,128]{2,1,0:T(8,128)S(1)} %get-tuple-element.107), custom_call_target="InvertDiagBlocksLowerTriangular" | custom-call | tf_op jit(solution)/shard_map/jit(cholesky)/cholesky | solution.py:40
  529.7 11.7 %cholesky.333 = f32[128,128]{1,0:T(8,128)S(1)} custom-call(f32[128,128]{1,0:T(8,128)S(1)} %convolution_subtract_fusion.4), custom_call_target="Cholesky" | custom-call | tf_op jit(solution)/shard_map/jit(cholesky)/cholesky | solution.py:40
  545.4 4.0 while.11
  546.0 1.4 bitcast_dynamic-update-slice_fusion.33
  550.1 20.5 %custom-call.24 = f32[2,128,128]{1,2,0:T(8,128)S(1)} custom-call(f32[2,128,128]{2,1,0:T(8,128)} %copy-done.34), custom_call_target="InvertDiagBlocksLowerTriangular" | custom-call | tf_op jit(solution)/shard_map/jit(_solve_triangular)/triangular_solve | solution.py:41
  572.8 2.5 convolution_bitcast_fusion
  (207 shorter events, 60.2 us)
Async XLA Ops:
  7.2 99.9 %copy-start = (f32[1024,256]{1,0:T(8,128)S(1)}, f32[1024,256]{1,0:T(8,128)}, u32[]{:S(2)}) copy-start(f32[1024,256]{1,0:T(8,128)} %param.7) | copy-start | bytes 3145732
  7.2 218.2 %all-reduce.3.cloned.1.call-start = ((), (), s32[]{:S(2)}) async-start(), calls=%async_computation.1 | async-start | bytes 4718592 | tf_op jit(solution)/shard_map/psum | solution.py:35
  226.5 37.6 %slice-start = ((f32[128,4608]{1,0:T(8,128)}), f32[128,896]{1,0:T(8,128)S(1)}, s32[]{:S(2)}) async-start(f32[128,4608]{1,0:T(8,128)} %all-reduce.3.cloned.1.call-done), calls=%async_computation.2 | async-start | bytes 917504 | tf_op jit(solution)/shard_map/slice | solution.py:23
  230.5 34.6 %slice-start.1 = ((f32[128,4608]{1,0:T(8,128)}), f32[128,768]{1,0:T(8,128)S(1)}, s32[]{:S(2)}) async-start(f32[128,4608]{1,0:T(8,128)} %all-reduce.3.cloned.1.call-done), calls=%async_computation.3 | async-start | bytes 786432 | tf_op jit(solution)/shard_map/slice | solution.py:23
  232.9 33.1 %slice-start.2 = ((f32[128,4608]{1,0:T(8,128)}), f32[128,640]{1,0:T(8,128)S(1)}, s32[]{:S(2)}) async-start(f32[128,4608]{1,0:T(8,128)} %all-reduce.3.cloned.1.call-done), calls=%async_computation.4 | async-start | bytes 655360 | tf_op jit(solution)/shard_map/slice | solution.py:23
  262.7 3.4 copy-start.20
  262.7 3.4 copy-start.17
  262.7 3.5 copy-start.18
  262.7 3.5 copy-start.33
  262.7 3.5 copy-start.2
  262.7 3.5 copy-start.32
  262.7 3.5 copy-start.31
  262.8 3.6 copy-start.30
  262.8 3.6 copy-start.29
  262.8 3.6 copy-start.28
  262.8 3.6 copy-start.27
  262.8 3.6 copy-start.26
  264.0 2.4 copy-start.25
  264.0 2.4 copy-start.24
  264.1 2.5 copy-start.23
  264.1 2.5 copy-start.22
  264.1 2.5 copy-start.21
  264.1 2.5 copy-start.19
  264.1 2.5 copy-start.16
  264.1 2.6 copy-start.15
  264.1 2.6 copy-start.14
  264.1 2.6 copy-start.12
  264.1 2.6 copy-start.13
  264.2 4.6 copy-start.7
  266.8 2.0 copy-start.1
  275.8 0.7 copy-start.8
  312.5 2.0 copy-start.3
  319.5 0.7 copy-start.35
  352.2 0.7 copy-start.9
  388.4 2.6 copy-start.4
  396.0 0.7 copy-start.36
  428.8 0.7 copy-start.10
  465.1 2.7 copy-start.5
  472.8 0.7 copy-start.37
  505.3 0.7 copy-start.11
  541.5 2.9 copy-start.6
  549.4 0.7 copy-start.34
Sparse Core Ops, SparseCore 0:
  125.6 99.7 all-reduce.2
